TPU v7x, 256 devices: a whole 4x4x8 slice. The times are simulated.
256 devices in a mesh: dp: 32 (over y_lo, z, core), code: 8 (over x, y_hi).
Axes of the slice: x: 4, y: 4 (y_hi: 2, y_lo: 2; y = y_hi * 2 + y_lo), z: 8, core: 2. Of those that a mesh axis runs over, the one named last changes fastest.
Arguments:
- latents: bfloat16 [8192, 256], P('dp'), may hold values from -128 to 128
- grads: bfloat16 [8192, 256], P('dp'), may hold values from -6 to 6
- codebook: bfloat16 [131072, 256], P(('dp', 'code')), may hold values from -2 to 2
- hard_code: int32 [8192], P('dp'), may hold values from 0 to 131071
Outputs:
- grad_latents: float32 [8192, 256], P('dp')
- grad_codebook: float32 [131072, 256], P(('dp', 'code'))
All inputs are finite; a program needn't handle non-finite values.
Results may differ from a plain program's by a relative error of at most 0.0034.
Values may be sent and summed in bfloat16 or wider, within the bound.
A program may use at most 192 MiB of HBM per device.

v0:
```python
import math

import jax
import jax.numpy as jnp
from jax import lax
from jax.sharding import PartitionSpec as P


def block_terms(stacked, rows, count):
    both = lax.dot_general(
        stacked, rows, (((1,), (1,)), ((), ())), preferred_element_type=jnp.float32
    )
    return (both[:count], both[count:])


def combine_parts(first, second):
    top = jnp.maximum(first[0], second[0])
    lower = jnp.exp(first[0] - top)
    upper = jnp.exp(second[0] - top)
    return (top, first[1] * lower + second[1] * upper, first[2] * lower + second[2] * upper)


def local_stats(stacked, count, table, width):
    groups = table.shape[0] // width

    def local_visit(carry, index):
        rows = lax.dynamic_slice_in_dim(table, index * width, width, 0)
        logit, pull = block_terms(stacked, rows, count)
        top = jnp.max(logit, axis=1)
        expo = jnp.exp(logit - top[:, None])
        return (
            combine_parts(carry, (top, jnp.sum(expo, axis=1), jnp.sum(expo * pull, axis=1))),
            None,
        )

    start = (
        jnp.full((count,), -1e30, jnp.float32),
        jnp.zeros((count,), jnp.float32),
        jnp.zeros((count,), jnp.float32),
    )
    result, unused = lax.scan(local_visit, start, jnp.arange(groups))
    return result


def soft_grad(logit, pull, top, total, mean_pull):
    probs = jnp.exp(logit - top[:, None]) / total[:, None]
    return (probs * (pull - mean_pull[:, None])).astype(jnp.bfloat16)


def per_device(latents, grads, codebook, hard_code):
    count = latents.shape[0]
    width_d = latents.shape[1]
    rows_dev = codebook.shape[0]
    n_code = lax.axis_size("code")
    code_pos = lax.axis_index("code")
    gathered = lax.all_gather(codebook, "dp", axis=0, tiled=True)
    stacked = jnp.concatenate([latents, grads], axis=0)
    width = math.gcd(gathered.shape[0], 512)
    part_top, part_total, part_weighted = local_stats(stacked, count, gathered, width)
    top = lax.pmax(part_top, "code")
    factor = jnp.exp(part_top - top)
    total, weighted = lax.psum((part_total * factor, part_weighted * factor), "code")
    mean_pull = weighted / total
    groups = gathered.shape[0] // width

    def body_visit(acc, index):
        rows = lax.dynamic_slice_in_dim(gathered, index * width, width, 0)
        logit, pull = block_terms(stacked, rows, count)
        dlogits = soft_grad(logit, pull, top, total, mean_pull)
        acc = acc + jnp.dot(dlogits, rows, preferred_element_type=jnp.float32)
        part = lax.dot_general(
            dlogits, latents, (((0,), (0,)), ((), ())), preferred_element_type=jnp.float32
        )
        return (acc, part)

    partial_latents, parts = lax.scan(
        body_visit, jnp.zeros((count, width_d), jnp.float32), jnp.arange(groups)
    )
    owner = hard_code // rows_dev
    mine = owner % n_code == code_pos
    slot = jnp.where(mine, owner // n_code * rows_dev + hard_code % rows_dev, gathered.shape[0])
    terms = parts.reshape(gathered.shape[0], width_d)
    terms = terms.at[slot].add(grads.astype(jnp.float32), mode="drop")
    grad_latents = lax.psum(partial_latents, "code")
    grad_codebook = lax.psum_scatter(terms, "dp", scatter_dimension=0, tiled=True)
    return (grad_latents, grad_codebook)


def solution(mesh):
    return jax.shard_map(
        per_device,
        mesh=mesh,
        in_specs=(P("dp", None), P("dp", None), P(("dp", "code"), None), P("dp")),
        out_specs=(P("dp", None), P(("dp", "code"), None)),
        check_vma=False,
    )
```

profile of v0, /device:TPU:32, one launch (start us, length us, event | category | flops | bytes accessed | tf_op | source)
XLA Modules:
  0.0 613.8 jit_solution(1165249163367299397)
XLA Ops:
  9.8 74.7 %all-gather.2.cloned.1.call-done = bf16[16384,256]{1,0:T(8,128)(2,1)} async-done(((bf16[512,256]{1,0:T(8,128)(2,1)}), bf16[16384,256]{1,0:T(8,128)(2,1)}) %all-gather.2.cloned.1.call-update) | async-done | bytes 8388624 | tf_op jit(solution)/shard_map/all_gather | solution.py:56
  84.6 89.4 %while.28 = (s32[]{:T(128)}, f32[256]{0:T(256)S(1)}, f32[256]{0:T(256)S(1)}, f32[256]{0:T(256)S(1)}, s32[32]{0:T(128)S(1)}, /*index=5*/bf16[16384,256]{1,0:T(8,1...) while((s32[]{:T(128)}, f32[256]{0:T(256)S(1)}, ...), condition=%wide.region_4.5_spmd.clone, body=%wide.region_0.4_spmd.clone.sunk | while | flops 134876160 | bytes 3164342 | solution.py:41
  88.6 1.3 convolution_bitcast_fusion.5
  91.4 1.3 convolution_bitcast_fusion.5
  174.0 23.8 %pmax.7 = f32[256]{0:T(256)S(1)} all-reduce(f32[256]{0:T(256)S(1)} %get-tuple-element.94), channel_id=1, replica_groups=mesh['dp'=32,'code'=8] {'code'}, use_global_device_ids=true, to_apply=%region_5.6 | all-reduce | flops 256 | bytes 2048 | tf_op jit(solution)/shard_map/pmax | solution.py:60
  197.8 19.0 %all-reduce = (f32[256]{0:T(256)S(1)}, f32[256]{0:T(256)S(1)}) all-reduce(f32[256]{0:T(256)S(1)} %get-tuple-element.197, f32[256]{0:T(256)S(1)} %get-tuple-element.196), channel_id=1, replica_groups=mesh['dp'=32,'code'=8] {'code'}, use_global_device_ids=true, to_apply=%region_6.7 | all-reduce | flops 512 | bytes 4096 | tf_op jit(solution)/shard_map/psum | solution.py:62
  216.8 159.4 %while.29 = (s32[]{:T(128)}, f32[256,256]{1,0:T(8,128)S(1)}, f32[32,512,256]{2,1,0:T(8,128)}, s32[32]{0:T(128)S(1)}, bf16[16384,256]{1,0:T(8,128)(2,1)}, /*index...) while((s32[]{:T(128)}, f32[256,256]{1,0:T(8,128)S(1)}, ...), condition=%wide.region_9.10_spmd.clone, body=%wide.region_8.9_spmd.clone.sunk | while | flops 269221888 | bytes 4853457 | solution.py:76
  223.0 1.3 convolution_bitcast_fusion.6
  228.0 1.3 convolution_bitcast_fusion.6
  238.0 1.3 convolution_bitcast_fusion.6
  247.9 1.3 convolution_bitcast_fusion.6
  252.9 1.3 convolution_bitcast_fusion.6
  257.9 1.3 convolution_bitcast_fusion.6
  262.8 1.3 convolution_bitcast_fusion.6
  267.8 1.3 convolution_bitcast_fusion.6
  277.8 1.3 convolution_bitcast_fusion.6
  287.8 1.3 convolution_bitcast_fusion.6
  292.7 1.3 convolution_bitcast_fusion.6
  297.7 1.3 convolution_bitcast_fusion.6
  302.7 1.3 convolution_bitcast_fusion.6
  307.8 1.3 convolution_bitcast_fusion.6
  312.7 1.3 convolution_bitcast_fusion.6
  322.7 1.3 convolution_bitcast_fusion.6
  327.7 1.3 convolution_bitcast_fusion.6
  347.6 1.3 convolution_bitcast_fusion.6
  357.6 1.3 convolution_bitcast_fusion.6
  367.5 1.3 convolution_bitcast_fusion.6
  372.5 1.3 convolution_bitcast_fusion.6
  377.0 13.3 %scatter_custom_fusion = f32[16384,256]{1,0:T(8,128)} fusion(f32[16384,256]{1,0:T(8,128)} %bitcast.36, s32[256]{0:T(256)S(1)} %compare_select_fusion, bf16[256,256]{1,0:T(8,128)(2,1)S(1)} %copy-done.2), kind=kCustom, calls=%fused_computation.31 | custom fusion | flops 131072 | bytes 16908288 | tf_op jit(solution)/shard_map/scatter-add | solution.py:83
  390.3 74.7 %all-reduce.3.cloned.1.call-done = f32[256,256]{1,0:T(8,128)} async-done(((f32[256,256]{1,0:T(8,128)}), f32[256,256]{1,0:T(8,128)}) %all-reduce.3.cloned.1.call-update) | async-done | bytes 262160 | tf_op jit(solution)/shard_map/psum | solution.py:84
  465.0 140.6 %reduce-scatter.2.cloned.1.call-done = f32[512,256]{1,0:T(8,128)} async-done(((f32[16384,256]{1,0:T(8,128)}), f32[512,256]{1,0:T(8,128)}) %reduce-scatter.2.cloned.1.call-update) | async-done | bytes 524304 | tf_op jit(solution)/shard_map/reduce_scatter | solution.py:85
  605.6 1.7 copy.31
  (387 shorter events, 179.4 us)
Async XLA Ops:
  7.2 209.6 %copy-start.1 = (bf16[256,256]{1,0:T(8,128)(2,1)S(1)}, bf16[256,256]{1,0:T(8,128)(2,1)}, u32[]{:S(2)}) copy-start(bf16[256,256]{1,0:T(8,128)(2,1)} %param.8) | copy-start | bytes 393220
  7.2 77.4 %all-gather.2.cloned.1.call-start = ((), (), s32[]{:S(2)}) async-start(), calls=%async_computation.1 | async-start | bytes 8650752 | tf_op jit(solution)/shard_map/all_gather | solution.py:56
  7.9 457.1 %all-reduce.3.cloned.1.call-start = ((), (), s32[]{:S(2)}) async-start(), calls=%async_computation.2 | async-start | bytes 524288 | tf_op jit(solution)/shard_map/psum | solution.py:84
  84.6 292.4 %copy-start.3 = (s32[256]{0:T(256)S(1)}, s32[256]{0:T(256)}, u32[]{:S(2)}) copy-start(s32[256]{0:T(256)} %param.11) | copy-start | bytes 3076
  84.6 292.5 %copy-start.2 = (bf16[256,256]{1,0:T(8,128)(2,1)S(1)}, bf16[256,256]{1,0:T(8,128)(2,1)}, u32[]{:S(2)}) copy-start(bf16[256,256]{1,0:T(8,128)(2,1)} %param.9) | copy-start | bytes 393220
  376.2 0.7 copy-start
  376.9 228.6 %reduce-scatter.2.cloned.1.call-start = ((), (), s32[]{:S(2)}) async-start(), calls=%async_computation.3 | async-start | bytes 17301504 | tf_op jit(solution)/shard_map/reduce_scatter | solution.py:85
Sparse Core Ops, SparseCore 0:
  9.9 74.6 all-gather.1
  377.1 87.8 all-reduce.2
  468.3 137.2 reduce-scatter.1
where the time goes:
time: 622 us; the launch traced here: 614 us
  waiting for transfers between devices  291 us (47%)
  matrix products  156 us (25%)
  loops' own time  43.4 us (7%)
  blocking collectives  42.8 us (7%)
  local copies, waits for them, and re-layouts  42.2 us (7%)
  other arithmetic  25.2 us (4%)
  between operations  13.8 us (2%)
    reduce_scatter x1, waiting for transfers between devices, per_device(): lax.psum_scatter(terms, 'dp', scatter_dimension=0, tiled=True)  141 us
    dot_general x64, matrix products, block_terms(): lax.dot_general(stacked, rows, (((1,), (1,)), ((), ())), preferred_elemen...  81.9 us
    all_gather x1, waiting for transfers between devices, per_device(): gathered = lax.all_gather(codebook, 'dp', axis=0, tiled=True)  74.7 us
    psum x1, waiting for transfers between devices, per_device(): grad_latents = lax.psum(partial_latents, 'code')  74.7 us
    dot_general x32, matrix products, body_visit(): acc = acc + jnp.dot(dlogits, rows, preferred_element_type=jnp.float32)  40.2 us
    dynamic_slice x64, local copies, waits for them, and re-layouts, local_stats(): result, unused = lax.scan(local_visit, start, jnp.arange(groups))  37.9 us
    dot_general x32, matrix products, body_visit(): lax.dot_general(dlogits, latents, (((0,), (0,)), ((), ())), preferred_ele...  33.5 us
    pmax x1, blocking collectives, per_device(): top = lax.pmax(part_top, 'code')  23.8 us
  transfers between devices with their start and end apart: 3, of which 3 were waited for; matrix products, arithmetic and copies ran while one was open for 2% of the time, Pallas kernels for 0%

commit v1 on v0

v1 whole, which is shorter than its diff:
```python
import functools

import jax
import jax.numpy as jnp
from jax import lax
from jax.experimental import pallas as pl
from jax.experimental.pallas import tpu as pltpu
from jax.sharding import PartitionSpec as P

MESH = pl.DeviceIdType.MESH
F32 = jnp.float32
BF16 = jnp.bfloat16

NX, NY, NZ, NC = 4, 4, 8, 2

S_X = 0
S_P = 4
S_M = 9
S_YA = 14
S_YB = 19
S_C = 24
S_ST1 = 44
S_ST2 = 52
S_ST3 = 60
S_GC = 68
S_GY = 72
S_GZ = 76
S_AG = 84
S_GX = 92
S_ALL = 96


def device(x, y, z, c):
    return ((y % 2 * NZ + z) * NC + c, x * 2 + y // 2)


def nt_dot(a, b):
    return lax.dot_general(a, b, (((1,), (1,)), ((), ())), preferred_element_type=F32)


def kernel(
    lat, gr, cb, hc, olat, ocb,
    LAT, GR, HC, CB, CBT, E, PU, D, MB, ST, ST1, ST2, FIN,
    GCT, GCR, GYK, GYT, GYR, GZK, GZT, GZR, GA, GXT, GXR,
    ss, rs,
):
    T = lat.shape[0]
    K = cb.shape[0]
    half = T // 2
    part = T // NZ
    dp = lax.axis_index("dp")
    code = lax.axis_index("code")
    c = dp % NC
    z = dp // NC % NZ
    yl = dp // (NC * NZ)
    x = code // 2
    yh = code % 2
    y = yh * 2 + yl
    a = (z - x + NZ) % NZ

    def at(dx=0, dy=0, dz=0, dc=0):
        return device((x + dx) % NX, (y + dy) % NY, (z + dz) % NZ, (c + dc) % NC)

    def copy(src, dst, dev, i, j=None):
        return pltpu.make_async_remote_copy(
            src_ref=src, dst_ref=dst, send_sem=ss.at[i], recv_sem=rs.at[i if j is None else j],
            device_id=dev, device_id_type=MESH,
        )

    def send(src, dst, dev, i, j=None):
        copy(src, dst, dev, i, j).start()

    def recv(dst, i):
        copy(dst, dst, at(dc=1), i).wait_recv()

    def sent(src, i):
        copy(src, src, at(dc=1), i).wait_send()

    yc = [(dy, dc) for dc in range(NC) for dy in range(NY) if dy or dc]

    barrier = pltpu.get_barrier_semaphore()

    def greet(dev):
        pl.semaphore_signal(barrier, inc=1, device_id=dev, device_id_type=MESH)

    for d in range(1, NX):
        greet(at(dx=d))
    for dy, dc in yc:
        greet(at(dy=dy, dc=dc))
    for d in range(1, NZ):
        greet(at(dz=d))
    home = z == x + NX * yh
    for zs in range(NZ):
        @pl.when(jnp.logical_not(home & (z == zs)))
        def _(zs=zs):
            greet(device(z % NX, z // NX * 2 + yl, zs, c))

    peers = NX - 1 + len(yc) + NZ - 1 + 8
    pl.semaphore_wait(barrier, jnp.where(home, peers - 1, peers))

    send(cb, CB.at[x], at(dx=1), S_X)
    send(cb, CB.at[x], at(dx=NX - 1), S_X + 1)

    def chunk(c_, yl_, b_):
        return (c_ * 2 + yl_) * 2 + b_

    def pieces(q):
        for arr in (LAT, GR):
            for h in range(2):
                yield arr.at[pl.ds(pl.multiple_of(q * T + h * half, half), half)]
        yield HC.at[q]

    b_own = a // NX
    q_own = chunk(c, yl, b_own)
    b_sp = a // NX
    b_rp = (a + NZ - 1) % NZ // NX
    b_sm = (NZ - a) % NZ // NX
    b_rm = (2 * NZ - 1 - a) % NZ // NX
    source = a % NX == 0
    last = a % NX == 1

    @pl.when(source)
    def _():
        rows = pl.ds(pl.multiple_of(q_own * T, T), T)
        LAT[rows, :] = lat[...]
        GR[rows, :] = gr[...]
        HC[q_own] = hc[...]
        for p, piece in enumerate(pieces(q_own)):
            send(piece, piece, at(dz=1), S_P + p)
            send(piece, piece, at(dz=NZ - 1), S_M + p)

    CB[x] = cb[...]

    sp = list(pieces(chunk(c, yl, b_sp)))
    sm = list(pieces(chunk(c, yl, b_sm)))
    rp = list(pieces(chunk(c, yl, b_rp)))
    rm = list(pieces(chunk(c, yl, b_rm)))
    pa = list(pieces(chunk(c, yl, 0)))
    pb = list(pieces(chunk(c, yl, 1)))
    oa = list(pieces(chunk(c, 1 - yl, 0)))
    ob = list(pieces(chunk(c, 1 - yl, 1)))
    for p in range(5):
        recv(rp[p], S_P + p)

        @pl.when(jnp.logical_not(source))
        def _(p=p):
            send(rp[p], rp[p], at(dz=1), S_P + p)
            recv(rm[p], S_M + p)

            @pl.when(jnp.logical_not(last))
            def _():
                send(rm[p], rm[p], at(dz=NZ - 1), S_M + p)

        send(pa[p], pa[p], at(dy=1), S_YA + p)
        send(pb[p], pb[p], at(dy=NY - 1), S_YB + p)
        send(pa[p], pa[p], at(dc=1), S_C + p)
        send(pb[p], pb[p], at(dc=1), S_C + 5 + p)
        if p == 2:
            left = (x + NX - 1) % NX
            right = (x + 1) % NX
            far = (x + 2) % NX
            recv(CB.at[left], S_X)
            send(CB.at[left, pl.ds(0, K // 2)], CB.at[left, pl.ds(0, K // 2)], at(dx=1), S_X + 2)
            recv(CB.at[right], S_X + 1)
            send(CB.at[right, pl.ds(K // 2, K // 2)], CB.at[right, pl.ds(K // 2, K // 2)], at(dx=NX - 1), S_X + 3)
    for p in range(5):
        recv(oa[p], S_YA + p)
        send(oa[p], oa[p], at(dc=1), S_C + 10 + p)
        recv(ob[p], S_YB + p)
        send(ob[p], ob[p], at(dc=1), S_C + 15 + p)
    recv(CB.at[far, pl.ds(0, K // 2)], S_X + 2)
    recv(CB.at[far, pl.ds(K // 2, K // 2)], S_X + 3)
    other = [
        list(pieces(chunk(1 - c, yl_, b_)))
        for yl_, b_ in ((yl, 0), (yl, 1), (1 - yl, 0), (1 - yl, 1))
    ]
    for k in range(4):
        for p in range(5):
            recv(other[k][p], S_C + 5 * k + p)

    for j in range(NX):
        CBT[:, j * K:(j + 1) * K] = CB[j].T

    def first(q, carry):
        rows = pl.ds(pl.multiple_of(q * T, T), T)

        def inner(j, stats):
            top_old, total_old, weighted_old = stats
            codes = CB[j]
            logit = nt_dot(codes, LAT[rows, :])
            pull = nt_dot(codes, GR[rows, :])
            top = jnp.max(logit, axis=0, keepdims=True)
            expo = jnp.exp(logit - top)
            E[q, j] = expo
            PU[q, j] = pull
            MB[q, j] = jnp.broadcast_to(top, (8, T))
            total = jnp.sum(expo, axis=0, keepdims=True)
            weighted = jnp.sum(expo * pull, axis=0, keepdims=True)
            return merge((top_old, total_old, weighted_old), (top, total, weighted))

        start = (jnp.full((1, T), -1e30, F32), jnp.zeros((1, T), F32), jnp.zeros((1, T), F32))
        top, total, weighted = lax.fori_loop(0, NX, inner, start)
        ST[q] = jnp.concatenate([top, total, weighted, jnp.zeros((5, T), F32)], axis=0)
        return carry

    def merge(one, two):
        top = jnp.maximum(one[0], two[0])
        low = jnp.exp(one[0] - top)
        high = jnp.exp(two[0] - top)
        return (top, one[1] * low + two[1] * high, one[2] * low + two[2] * high)

    def merge_all(terms):
        total = None
        for t in terms:
            rows = (t[0:1], t[1:2], t[2:3])
            total = rows if total is None else merge(total, rows)
        return total

    def pack(rows):
        return jnp.concatenate([*rows, jnp.zeros((5, T), F32)], axis=0)

    lax.fori_loop(0, 8, first, 0)

    def mine(y_, c_):
        return chunk(c_, y_ % 2, y_ // 2)

    q_me = mine(y, c)
    for dy, dc in yc:
        n = dc * NY + dy
        send(ST.at[mine((y + dy) % NY, (c + dc) % NC)], ST1.at[n], at(dy=dy, dc=dc), S_ST1 + n)
    for dy, dc in yc:
        recv(ST1.at[dc * NY + dy], S_ST1 + dc * NY + dy)
    ST2[0] = pack(merge_all([ST[q_me]] + [ST1[dc * NY + dy] for dy, dc in yc]))
    for d in range(1, NZ):
        send(ST2.at[0], ST2.at[d], at(dz=d), S_ST2 + d)
    for d in range(1, NZ):
        recv(ST2.at[d], S_ST2 + d)
    top, total, weighted = merge_all([ST2[d] for d in range(NZ)])
    FIN[q_me] = pack((top, 1.0 / total, weighted / total))
    for dy, dc in yc:
        n = dc * NY + dy
        send(FIN.at[q_me], FIN.at[q_me], at(dy=dy, dc=dc), S_ST3 + n)
    for dy, dc in yc:
        recv(FIN.at[mine((y + NY - dy) % NY, (c + dc) % NC)], S_ST3 + dc * NY + dy)

    def latent_grad(q):
        fin = FIN[q]
        cols = pl.ds(pl.multiple_of(q * T, T), T)

        def inner(j, carry):
            factor = jnp.exp(MB[q, j][0:1] - fin[0:1]) * fin[1:2]
            dlog = (E[q, j] * factor) * (PU[q, j] - fin[2:3])
            D[pl.ds(pl.multiple_of(j * K, K), K), cols] = dlog.astype(BF16)
            return carry

        lax.fori_loop(0, NX, inner, 0)
        return jnp.dot(CBT[...], D[:, cols], preferred_element_type=F32).T

    def for_other(k, carry):
        GCT[k] = latent_grad((1 - c) * 4 + k)
        send(GCT.at[k], GCR.at[k], at(dc=1), S_GC + k)
        return carry

    lax.fori_loop(0, 4, for_other, 0)

    def for_own(d, carry):
        y_ = (y + d) % NY
        k = y_ % 2 * 2 + y_ // 2
        total = latent_grad(c * 4 + k)
        recv(GCR.at[k], S_GC + k)
        total = total + GCR[k]

        @pl.when(d == 0)
        def _():
            GYK[...] = total

        @pl.when(d > 0)
        def _():
            GYT[d] = total.astype(BF16)
            send(GYT.at[d], GYR.at[d], at(dy=d), S_GY + d)

        return carry

    lax.fori_loop(0, 4, for_own, 0)

    base = ((yl * NZ + z) * NC + c) * 8 + yh

    def codebook_grad(d):
        j = (x + d) % NX
        first_code = (base + j * 2) * K
        acc = jnp.dot(D[pl.ds(pl.multiple_of(j * K, K), K), :], LAT[...], preferred_element_type=F32)
        ids = first_code + lax.broadcasted_iota(jnp.int32, (K, T), 0)
        for q in range(8):
            hit = jnp.where(HC[q][0:1] == ids, 1.0, 0.0).astype(BF16)
            acc = acc + jnp.dot(hit, GR[q * T:(q + 1) * T, :], preferred_element_type=F32)
        return acc

    def codebook_send(d):
        GXT[d] = codebook_grad(d).astype(BF16)
        send(GXT.at[d], GXR.at[d], at(dx=d), S_GX + d)

    codebook_send(2)

    total = GYK[...]
    for d in range(1, NY):
        recv(GYR.at[d], S_GY + d)
        total = total + GYR[d].astype(F32)
    GZK[...] = total
    GZT[...] = total.astype(BF16)
    for d in range(1, NZ):
        rows = pl.ds(pl.multiple_of((z + d) % NZ * part, part), part)
        send(GZT.at[rows], GZR.at[d], at(dz=d), S_GZ + d)

    codebook_send(1)
    codebook_send(3)

    total = GZK[pl.ds(pl.multiple_of(z * part, part), part), :]
    for d in range(1, NZ):
        recv(GZR.at[d], S_GZ + d)
        total = total + GZR[d].astype(F32)
    GA[...] = total
    dst = olat.at[pl.ds(pl.multiple_of(z * part, part), part)]
    for dx in range(NX):
        for dh in range(2):
            dev = device((x + dx) % NX, (yh + dh) % 2 * 2 + yl, x + NX * yh, c)
            if dx or dh:
                send(GA, dst, dev, S_AG + dx * 2 + dh, S_AG + z)
            else:
                @pl.when(jnp.logical_not(home))
                def _(dev=dev):
                    send(GA, dst, dev, S_AG, S_AG + z)

                @pl.when(home)
                def _():
                    olat[pl.ds(pl.multiple_of(z * part, part), part), :] = GA[...]

    total = codebook_grad(0)
    for d in range(1, NX):
        recv(GXR.at[d], S_GX + d)
        total = total + GXR[d].astype(F32)
    ocb[...] = total

    for zs in range(NZ):
        @pl.when(jnp.logical_not(home & (z == zs)))
        def _(zs=zs):
            recv(olat.at[pl.ds(zs * part, part)], S_AG + zs)

    sent(cb, S_X)
    sent(cb, S_X + 1)
    sent(CB.at[0, pl.ds(0, K // 2)], S_X + 2)
    sent(CB.at[0, pl.ds(0, K // 2)], S_X + 3)
    for p in range(5):
        sent(sp[p], S_P + p)

        @pl.when(jnp.logical_not(last))
        def _(p=p):
            sent(sm[p], S_M + p)

        sent(pa[p], S_YA + p)
        sent(pb[p], S_YB + p)
        for k, own in enumerate((pa, pb, oa, ob)):
            sent(own[p], S_C + 5 * k + p)
    for dy, dc in yc:
        n = dc * NY + dy
        sent(ST.at[0], S_ST1 + n)
        sent(FIN.at[0], S_ST3 + n)
    for d in range(1, NZ):
        sent(ST2.at[0], S_ST2 + d)
        sent(GZT.at[pl.ds(0, part)], S_GZ + d)
    for k in range(4):
        sent(GCT.at[k], S_GC + k)
    for d in range(1, NY):
        sent(GYT.at[d], S_GY + d)
    for d in range(1, NX):
        sent(GXT.at[d], S_GX + d)
    for n in range(1, 8):
        sent(GA, S_AG + n)

    @pl.when(jnp.logical_not(home))
    def _():
        sent(GA, S_AG)


def per_device(latents, grads, codebook, hard_code):
    T, W = latents.shape
    K = codebook.shape[0]
    part = T // NZ
    vmem = pl.BlockSpec(memory_space=pltpu.VMEM)
    hc = jnp.broadcast_to(hard_code[None, :], (8, T))
    scratch = [
        ((8 * T, W), BF16),
        ((8 * T, W), BF16),
        ((8, 8, T), jnp.int32),
        ((NX, K, W), BF16),
        ((W, NX * K), BF16),
        ((8, NX, K, T), F32),
        ((8, NX, K, T), F32),
        ((NX * K, 8 * T), BF16),
        ((8, NX, 8, T), F32),
        ((8, 8, T), F32),
        ((8, 8, T), F32),
        ((8, 8, T), F32),
        ((8, 8, T), F32),
        ((4, T, W), F32),
        ((4, T, W), F32),
        ((T, W), F32),
        ((4, T, W), BF16),
        ((4, T, W), BF16),
        ((T, W), F32),
        ((T, W), BF16),
        ((NZ, part, W), BF16),
        ((part, W), F32),
        ((NX, K, W), BF16),
        ((NX, K, W), BF16),
    ]
    return pl.pallas_call(
        kernel,
        out_shape=(jax.ShapeDtypeStruct((T, W), F32), jax.ShapeDtypeStruct((K, W), F32)),
        in_specs=[vmem] * 4,
        out_specs=(vmem, vmem),
        scratch_shapes=[pltpu.VMEM(s, t) for s, t in scratch]
        + [pltpu.SemaphoreType.DMA((S_ALL,)), pltpu.SemaphoreType.DMA((S_ALL,))],
        compiler_params=pltpu.CompilerParams(
            collective_id=0, has_side_effects=True, vmem_limit_bytes=60 * 2**20
        ),
    )(latents, grads, codebook, hc)


def solution(mesh):
    return jax.shard_map(
        per_device,
        mesh=mesh,
        in_specs=(P("dp", None), P("dp", None), P(("dp", "code"), None), P("dp")),
        out_specs=(P("dp", None), P(("dp", "code"), None)),
        check_vma=False,
    )
```

time: 622 us -> 171 us (0.27); the launches traced: 614 us -> 170 us
  waiting for transfers between devices: 291 us -> 0 us
  Pallas kernels: 0 us -> 165 us
  matrix products: 156 us -> 0 us
  loops' own time: 43.4 us -> 0 us
  blocking collectives: 42.8 us -> 0 us
  local copies, waits for them, and re-layouts: 42.2 us -> 3.8 us
  other arithmetic: 25.2 us -> 0 us
  between operations: 13.8 us -> 0.65 us
    pallas_call x0 -> x1, Pallas kernels: none -> 165 us  [per_device(): pl.pallas_call(kernel, out_shape=(jax.ShapeDtypeStruct((T, W), F32), jax....]
    dot_general x128 -> x0, matrix products: 156 us -> none  [the longest x64 81.9 us: block_terms(): lax.dot_general(stacked, rows, (((1,), (1,)), ((), ())), preferred_elemen...]
    reduce_scatter x1 -> x0, waiting for transfers between devices: 141 us -> none  [per_device(): lax.psum_scatter(terms, 'dp', scatter_dimension=0, tiled=True)]
    all_gather x1 -> x0, waiting for transfers between devices: 74.7 us -> none  [per_device(): gathered = lax.all_gather(codebook, 'dp', axis=0, tiled=True)]
    psum x1 -> x0, waiting for transfers between devices: 74.7 us -> none  [per_device(): grad_latents = lax.psum(partial_latents, 'code')]
    another operation x2 -> x0, loops' own time: 43.4 us -> none  [the longest x1 22.1 us: per_device(): lax.scan(body_visit, jnp.zeros((count, width_d), jnp.float32), jnp.arange...]
    dynamic_slice x64 -> x0, local copies, waits for them, and re-layouts: 37.9 us -> none  [local_stats(): result, unused = lax.scan(local_visit, start, jnp.arange(groups))]
    pmax x1 -> x0, blocking collectives: 23.8 us -> none  [per_device(): top = lax.pmax(part_top, 'code')]
  transfers between devices with their start and end apart: 3 -> 0, of which waited for: 3 -> 0; matrix products, arithmetic and copies ran while one was open for 2% -> 0% of each run, Pallas kernels for 0% -> 0%
where the time goes in v1:
time: 171 us; the launch traced here: 170 us
  Pallas kernels  165 us (96%)
  local copies, waits for them, and re-layouts  3.8 us (2%)
    pallas_call x1, Pallas kernels, per_device(): pl.pallas_call(kernel, out_shape=(jax.ShapeDtypeStruct((T, W), F32), jax....  165 us

profile of v1, /device:TPU:32, one launch (start us, length us, event | category | flops | bytes accessed | tf_op | source)
XLA Modules:
  0.0 169.7 jit_solution(11383500065497003163)
XLA Ops:
  0.6 1.3 broadcast_in_dim.2.hc
  1.9 165.3 %shard_map.59 = (f32[256,256]{1,0:T(8,128)}, f32[512,256]{1,0:T(8,128)}) custom-call(bf16[256,256]{1,0:T(8,128)(2,1)} %lat.1, bf16[256,256]{1,0:T(8,128)(2,1)} %gr.1, bf16[512,256]{1,0:T(8,128)(2,1)} %cb.1, s32[8,256]{1,0:T(8,128)} %broadcast_in_dim.2.hc), custom_call_target="tpu_custom_call" | custom-call | tf_op jit(solution)/shard_map/pallas_call | solution.py:416
  167.2 0.0 copy-start
  167.2 1.7 %copy.8 = f32[256,256]{1,0:T(8,128)} copy(f32[256,256]{1,0:T(8,128)} %get-tuple-element.4) | data formatting | bytes 524288
  168.9 0.0 copy-done
  168.9 0.8 copy.9
Async XLA Ops:
  167.2 1.7 %copy-start = (f32[512,256]{1,0:T(8,128)S(1)}, f32[512,256]{1,0:T(8,128)}, u32[]{:S(2)}) copy-start(f32[512,256]{1,0:T(8,128)} %get-tuple-element.5) | copy-start | bytes 1572868

commit v2 on v1

v2 whole, which is shorter than its diff:
```python
import functools

import jax
import jax.numpy as jnp
from jax import lax
from jax.experimental import pallas as pl
from jax.experimental.pallas import tpu as pltpu
from jax.sharding import PartitionSpec as P

MESH = pl.DeviceIdType.MESH
F32 = jnp.float32
BF16 = jnp.bfloat16

NX, NY, NZ, NC = 4, 4, 8, 2
STEP = 256

S_X = 0
S_Z = 4
S_YA = 14
S_YB = 19
S_C = 24
S_ST1 = 44
S_ST2 = 52
S_ST3 = 60
S_GC = 68
S_GY = 72
S_GZ = 76
S_AG = 84
S_GX = 92
S_ALL = 96


def device(x, y, z, c):
    return ((y % 2 * NZ + z) * NC + c, x * 2 + y // 2)


def xor4(a, b):
    return (a % 2 + b % 2) % 2 + 2 * ((a // 2 + b // 2) % 2)


def nt_dot(a, b):
    return lax.dot_general(a, b, (((1,), (1,)), ((), ())), preferred_element_type=F32)


def merge(one, two):
    top = jnp.maximum(one[0], two[0])
    low = jnp.exp(one[0] - top)
    high = jnp.exp(two[0] - top)
    return (top, one[1] * low + two[1] * high, one[2] * low + two[2] * high)


def merge_all(terms):
    total = None
    for t in terms:
        rows = (t[0:1], t[1:2], t[2:3])
        total = rows if total is None else merge(total, rows)
    return total


def pack(rows):
    return jnp.concatenate([*rows, jnp.zeros((5, rows[0].shape[1]), F32)], axis=0)


def kernel(
    lat, gr, cb, hc, olat, ocb,
    LAT, GR, HC, HCL, CB, CBT, E, PU, D, H, ST, ST1, ST2, FIN,
    GCT, GCR, GYK, GYT, GYR, GZT, GZR, GXT, GXR,
    ss, rs,
):
    T, W = lat.shape
    K = cb.shape[0]
    half = T // 2
    part = T // 8
    dp = lax.axis_index("dp")
    code = lax.axis_index("code")
    c = dp % NC
    z = dp // NC % NZ
    yl = dp // (NC * NZ)
    x = code // 2
    yh = code % 2
    y = yh * 2 + yl
    zb = z // 4
    zt = xor4(z % 4, x)

    def at(dx=0, dy=0, dz=0, dc=0):
        return device((x + dx) % NX, (y + dy) % NY, (z + dz) % NZ, (c + dc) % NC)

    def diag(dz):
        z_ = (z + dz) % NZ
        return device(xor4(x, xor4(z % 4, z_ % 4)), y, z_, c)

    def copy(src, dst, dev, i, j=None):
        return pltpu.make_async_remote_copy(
            src_ref=src, dst_ref=dst, send_sem=ss.at[i], recv_sem=rs.at[i if j is None else j],
            device_id=dev, device_id_type=MESH,
        )

    def send(src, dst, dev, i, j=None):
        copy(src, dst, dev, i, j).start()

    def recv(dst, i):
        copy(dst, dst, at(dc=1), i).wait_recv()

    def sent(src, i):
        copy(src, src, at(dc=1), i).wait_send()

    def codes(j, first=0, count=K):
        return pl.ds(pl.multiple_of(j * K + first, count), count)

    yc = [(dy, dc) for dc in range(NC) for dy in range(NY) if dy or dc]
    xh = [(dx, dh) for dx in range(NX) for dh in range(2)]

    def across(dx, dh):
        return device((x + dx) % NX, (yh + dh) % 2 * 2 + yl, z, c)

    barrier = pltpu.get_barrier_semaphore()

    def greet(dev):
        pl.semaphore_signal(barrier, inc=1, device_id=dev, device_id_type=MESH)

    away = [jnp.logical_not((x == 0) & (zb == b)) for b in range(2)]
    home = (x == 0) & (zb == yh)
    for d in range(1, NX):
        greet(at(dx=d))
    for dy, dc in yc:
        greet(at(dy=dy, dc=dc))
    for d in range(1, NZ):
        greet(diag(d))
    for dx, dh in xh[1:]:
        greet(across(dx, dh))
    for b in range(2):
        @pl.when(away[b])
        def _(b=b):
            greet(device(x, y, zt + 4 * b, c))
    for zs in range(NZ):
        @pl.when(jnp.logical_not(home & (z == zs)))
        def _(zs=zs):
            greet(device(xor4(zs % 4, z % 4), zb * 2 + yl, zs, c))

    peers = NX - 1 + len(yc) + NZ - 1 + 7 + 2 + 8
    peers = peers - jnp.where(x == 0, 1, 0) - jnp.where(home, 1, 0)
    pl.semaphore_wait(barrier, peers)

    def chunk(c_, yl_, b_):
        return (c_ * 2 + yl_) * 2 + b_

    def tokens(q):
        return pl.ds(pl.multiple_of(q * T, T), T)

    def pieces(q):
        for arr in (LAT, GR):
            for h in range(2):
                yield arr.at[pl.ds(pl.multiple_of(q * T + h * half, half), half)]
        yield HC.at[q]

    HCL[...] = jnp.broadcast_to(hc[...].reshape(1, T), (8, T))
    q_own = chunk(c, yl, zb)
    own = [arr.at[pl.ds(h * half, half)] for arr in (lat, gr) for h in range(2)] + [HCL]
    dst = list(pieces(q_own))
    for p in range(5):
        for b in range(2):
            @pl.when(away[b])
            def _(p=p, b=b):
                send(own[p], dst[p], device(x, y, zt + 4 * b, c), S_Z + b * 5 + p, S_Z + zb * 5 + p)
        if p == 1:
            send(cb, CB.at[codes(x)], at(dx=1), S_X)
            send(cb, CB.at[codes(x)], at(dx=NX - 1), S_X + 1)

    @pl.when(x == 0)
    def _():
        LAT[tokens(q_own), :] = lat[...]
        GR[tokens(q_own), :] = gr[...]
        HC[q_own] = HCL[...]

    CB[codes(x), :] = cb[...]

    order = [chunk(c_, yl_, b) for c_ in (c, 1 - c) for yl_ in (yl, 1 - yl) for b in range(2)]
    refs = [list(pieces(q)) for q in order]
    left = (x + NX - 1) % NX
    right = (x + 1) % NX
    far = (x + 2) % NX
    far_refs = [CB.at[codes(left, 0, K // 2)], CB.at[codes(right, K // 2, K // 2)]]
    for p in range(5):
        for b in range(2):
            ref = refs[b][p]

            @pl.when(away[b])
            def _(ref=ref, i=S_Z + b * 5 + p):
                recv(ref, i)

            send(ref, ref, at(dy=NY - 1 if b else 1), (S_YB if b else S_YA) + p)
            send(ref, ref, at(dc=1), S_C + 5 * b + p)
        if p == 1:
            recv(CB.at[codes(left)], S_X)
            send(far_refs[0], far_refs[0], at(dx=1), S_X + 2)
            recv(CB.at[codes(right)], S_X + 1)
            send(far_refs[1], far_refs[1], at(dx=NX - 1), S_X + 3)
    recv(CB.at[codes(far, 0, K // 2)], S_X + 2)
    recv(CB.at[codes(far, K // 2, K // 2)], S_X + 3)

    def first(n):
        q = order[n]
        logit = nt_dot(CB[...], LAT[tokens(q), :])
        E[n] = logit
        PU[n] = nt_dot(CB[...], GR[tokens(q), :])
        top = jnp.max(logit, axis=0, keepdims=True)

        def rows(i, sums):
            at_ = pl.ds(pl.multiple_of(i * STEP, STEP), STEP)
            expo = jnp.exp(E[n, at_, :] - top)
            E[n, at_, :] = expo
            weighted = expo * PU[n, at_, :]
            return (
                sums[0] + jnp.sum(expo.reshape(STEP // 8, 8, T), axis=0),
                sums[1] + jnp.sum(weighted.reshape(STEP // 8, 8, T), axis=0),
            )

        zero = jnp.zeros((8, T), F32)
        total, weighted = lax.fori_loop(0, NX * K // STEP, rows, (zero, zero))
        total = jnp.sum(total, axis=0, keepdims=True)
        ST[q] = pack((top, total, jnp.sum(weighted, axis=0, keepdims=True)))

    first(0)
    first(1)
    for p in range(5):
        for b in range(2):
            ref = refs[2 + b][p]
            recv(ref, (S_YB if b else S_YA) + p)
            send(ref, ref, at(dc=1), S_C + 10 + 5 * b + p)
    first(2)
    first(3)
    for k in range(4):
        for p in range(5):
            recv(refs[4 + k][p], S_C + 5 * k + p)
    for n in range(4, 8):
        first(n)

    base = ((yl * NZ + z) * NC + c) * 8 + yh

    def hard_rows(d):
        first_code = (base + (x + d) % NX * 2) * K
        ids = first_code + lax.broadcasted_iota(jnp.int32, (K, 8 * T), 0)
        row = jnp.concatenate([HC[q][0:1] for q in range(8)], axis=1)
        hit = jnp.where(row == ids, 1.0, 0.0).astype(BF16)
        H[d] = jnp.dot(hit, GR[...], preferred_element_type=F32)

    def mine(y_, c_):
        return chunk(c_, y_ % 2, y_ // 2)

    q_me = mine(y, c)
    for dy, dc in yc:
        n = dc * NY + dy
        send(ST.at[mine((y + dy) % NY, (c + dc) % NC)], ST1.at[n], at(dy=dy, dc=dc), S_ST1 + n)
    hard_rows(2)
    for dy, dc in yc:
        recv(ST1.at[dc * NY + dy], S_ST1 + dc * NY + dy)
    ST2[0] = pack(merge_all([ST[q_me]] + [ST1[dc * NY + dy] for dy, dc in yc]))
    for d in range(1, NZ):
        send(ST2.at[0], ST2.at[d], diag(d), S_ST2 + d)
    hard_rows(1)
    hard_rows(3)
    for d in range(1, NZ):
        recv(ST2.at[d], S_ST2 + d)
    top, total, weighted = merge_all([ST2[d] for d in range(NZ)])
    FIN[q_me] = pack((top, 1.0 / total, weighted / total))
    for dy, dc in yc:
        n = dc * NY + dy
        send(FIN.at[q_me], FIN.at[q_me], at(dy=dy, dc=dc), S_ST3 + n)
    hard_rows(0)
    CBT[...] = CB[...].T
    for dy, dc in yc:
        recv(FIN.at[mine((y + NY - dy) % NY, (c + dc) % NC)], S_ST3 + dc * NY + dy)

    def latent_grad(n, q):
        fin = FIN[q]
        factor = jnp.exp(ST[q][0:1] - fin[0:1]) * fin[1:2]
        dlog = ((E[n] * factor) * (PU[n] - fin[2:3])).astype(BF16)
        D[:, tokens(q)] = dlog
        return jnp.dot(CBT[...], dlog, preferred_element_type=F32).T

    for k in range(4):
        GCT[k] = latent_grad(4 + k, order[4 + k])
        send(GCT.at[k], GCR.at[k], at(dc=1), S_GC + k)

    for d in (2, 1, 3, 0):
        y_ = (y + d) % NY
        k = (y_ + yl) % 2 * 2 + y_ // 2
        total = latent_grad(k, mine(y_, c))
        if d == 2:
            for k_ in range(4):
                recv(GCR.at[k_], S_GC + k_)
        total = total + GCR[k]
        if d:
            GYT[d] = total.astype(BF16)
            send(GYT.at[d], GYR.at[d], at(dy=d), S_GY + d)
        else:
            GYK[...] = total

    def codebook_grad(d):
        return H[d] + jnp.dot(D[codes((x + d) % NX), :], LAT[...], preferred_element_type=F32)

    def codebook_send(d):
        GXT[d] = codebook_grad(d).astype(BF16)
        send(GXT.at[d], GXR.at[d], at(dx=d), S_GX + d)

    codebook_send(2)
    codebook_send(1)

    total = GYK[...]
    for d in range(1, NY):
        recv(GYR.at[d], S_GY + d)
        total = total + GYR[d].astype(F32)
    GZT[...] = total.astype(BF16)

    def rows_of(x_, yh_):
        return pl.ds(pl.multiple_of((x_ * 2 + yh_) * part, part), part)

    rows_me = rows_of(x, yh)
    for dx, dh in xh:
        x_ = (x + dx) % NX
        yh_ = (yh + dh) % 2
        src = GZT.at[rows_of(x_, yh_)]
        dev = device(x_, yh_ * 2 + yl, zt + 4 * yh, c)
        if dx or dh:
            send(src, GZR.at[z], dev, S_GZ + dx * 2 + dh, S_GZ + z)
        else:
            @pl.when(jnp.logical_not(home))
            def _(src=src, dev=dev):
                send(src, GZR.at[z], dev, S_GZ, S_GZ + z)

            @pl.when(home)
            def _():
                GZR[z] = GZT[rows_me, :]

    codebook_send(3)
    ocb[...] = codebook_grad(0)

    for zs in range(NZ):
        @pl.when(jnp.logical_not(home & (z == zs)))
        def _(zs=zs):
            recv(GZR.at[zs], S_GZ + zs)
    total = GZR[0].astype(F32)
    for zs in range(1, NZ):
        total = total + GZR[zs].astype(F32)
    olat[rows_me, :] = total
    for dx, dh in xh[1:]:
        ref = olat.at[rows_me]
        send(ref, ref, across(dx, dh), S_AG + dx * 2 + dh)

    total = ocb[...]
    for d in range(1, NX):
        recv(GXR.at[d], S_GX + d)
        total = total + GXR[d].astype(F32)
    ocb[...] = total

    for dx, dh in xh[1:]:
        recv(olat.at[rows_of((x + NX - dx) % NX, (yh + dh) % 2)], S_AG + dx * 2 + dh)

    sent(cb, S_X)
    sent(cb, S_X + 1)
    sent(far_refs[0], S_X + 2)
    sent(far_refs[1], S_X + 3)
    for p in range(5):
        for b in range(2):
            @pl.when(away[b])
            def _(p=p, b=b):
                sent(own[p], S_Z + b * 5 + p)

        sent(refs[0][p], S_YA + p)
        sent(refs[1][p], S_YB + p)
        for k in range(4):
            sent(refs[k][p], S_C + 5 * k + p)
    for dy, dc in yc:
        n = dc * NY + dy
        sent(ST.at[0], S_ST1 + n)
        sent(FIN.at[0], S_ST3 + n)
    for d in range(1, NZ):
        sent(ST2.at[0], S_ST2 + d)
    for k in range(4):
        sent(GCT.at[k], S_GC + k)
    for d in range(1, NY):
        sent(GYT.at[d], S_GY + d)
    for d in range(1, NX):
        sent(GXT.at[d], S_GX + d)
    for n in range(1, 8):
        sent(GZT.at[pl.ds(0, part)], S_GZ + n)
        sent(olat.at[pl.ds(0, part)], S_AG + n)

    @pl.when(jnp.logical_not(home))
    def _():
        sent(GZT.at[pl.ds(0, part)], S_GZ)


def per_device(latents, grads, codebook, hard_code):
    T, W = latents.shape
    K = codebook.shape[0]
    part = T // 8
    vmem = pl.BlockSpec(memory_space=pltpu.VMEM)
    scratch = [
        ((8 * T, W), BF16),
        ((8 * T, W), BF16),
        ((8, 8, T), jnp.int32),
        ((8, T), jnp.int32),
        ((NX * K, W), BF16),
        ((W, NX * K), BF16),
        ((8, NX * K, T), F32),
        ((8, NX * K, T), F32),
        ((NX * K, 8 * T), BF16),
        ((NX, K, W), F32),
        ((8, 8, T), F32),
        ((8, 8, T), F32),
        ((8, 8, T), F32),
        ((8, 8, T), F32),
        ((4, T, W), F32),
        ((4, T, W), F32),
        ((T, W), F32),
        ((4, T, W), BF16),
        ((4, T, W), BF16),
        ((T, W), BF16),
        ((NZ, part, W), BF16),
        ((NX, K, W), BF16),
        ((NX, K, W), BF16),
    ]
    return pl.pallas_call(
        kernel,
        out_shape=(jax.ShapeDtypeStruct((T, W), F32), jax.ShapeDtypeStruct((K, W), F32)),
        in_specs=[vmem] * 4,
        out_specs=(vmem, vmem),
        scratch_shapes=[pltpu.VMEM(s, t) for s, t in scratch]
        + [pltpu.SemaphoreType.DMA((S_ALL,)), pltpu.SemaphoreType.DMA((S_ALL,))],
        compiler_params=pltpu.CompilerParams(
            collective_id=0, has_side_effects=True, vmem_limit_bytes=62 * 2**20
        ),
    )(latents, grads, codebook, hard_code)


def solution(mesh):
    return jax.shard_map(
        per_device,
        mesh=mesh,
        in_specs=(P("dp", None), P("dp", None), P(("dp", "code"), None), P("dp")),
        out_specs=(P("dp", None), P(("dp", "code"), None)),
        check_vma=False,
    )
```

time: 171 us -> 90.5 us (0.53)
  Pallas kernels: 165 us -> 87.2 us
    pallas_call x1, Pallas kernels: 165 us -> 87.2 us  [per_device(): pl.pallas_call(kernel, out_shape=(jax.ShapeDtypeStruct((T, W), F32), jax....]
where the time goes in v2:
time: 90.5 us; the launch traced here: 90.3 us
  Pallas kernels  87.2 us (96%)
  local copies, waits for them, and re-layouts  2.52 us (3%)
    pallas_call x1, Pallas kernels, per_device(): pl.pallas_call(kernel, out_shape=(jax.ShapeDtypeStruct((T, W), F32), jax....  87.2 us
    unnamed x4, local copies, waits for them, and re-layouts  2.52 us

profile of v2, /device:TPU:32, one launch (start us, length us, event | category | flops | bytes accessed | tf_op | source)
XLA Modules:
  0.0 90.3 jit_solution(16676336649585450507)
XLA Ops:
  0.6 87.2 %shard_map.59 = (f32[256,256]{1,0:T(8,128)}, f32[512,256]{1,0:T(8,128)}) custom-call(bf16[256,256]{1,0:T(8,128)(2,1)} %lat.1, bf16[256,256]{1,0:T(8,128)(2,1)} %gr.1, bf16[512,256]{1,0:T(8,128)(2,1)} %cb.1, s32[256]{0:T(256)} %hc.1), custom_call_target="tpu_custom_call" | custom-call | tf_op jit(solution)/shard_map/pallas_call | solution.py:424
  87.8 0.0 copy-start
  87.8 1.7 %copy.8 = f32[256,256]{1,0:T(8,128)} copy(f32[256,256]{1,0:T(8,128)} %get-tuple-element.4) | data formatting | bytes 524288
  89.5 0.0 copy-done
  89.5 0.8 copy.9
Async XLA Ops:
  87.8 1.7 %copy-start = (f32[512,256]{1,0:T(8,128)S(1)}, f32[512,256]{1,0:T(8,128)}, u32[]{:S(2)}) copy-start(f32[512,256]{1,0:T(8,128)} %get-tuple-element.5) | copy-start | bytes 1572868

commit v3 on v2

v3 whole, which is shorter than its diff:
```python
import functools

import jax
import jax.numpy as jnp
from jax import lax
from jax.experimental import pallas as pl
from jax.experimental.pallas import tpu as pltpu
from jax.sharding import PartitionSpec as P

MESH = pl.DeviceIdType.MESH
F32 = jnp.float32
BF16 = jnp.bfloat16

NX, NY, NZ, NC = 4, 4, 8, 2
STEP = 256

S_X = 0
S_Z = 6
S_YA = 16
S_YB = 21
S_C = 26
S_SC = 46
S_SY = 48
S_SZ = 56
S_SF = 72
S_GC = 74
S_GY = 78
S_GZ = 86
S_AG = 102
S_GX = 118
S_ALL = 122


def device(x, y, z, c):
    return ((y % 2 * NZ + z) * NC + c, x * 2 + y // 2)


def xor4(a, b):
    return (a % 2 + b % 2) % 2 + 2 * ((a // 2 + b // 2) % 2)


def nt_dot(a, b):
    return lax.dot_general(a, b, (((1,), (1,)), ((), ())), preferred_element_type=F32)


def merge(terms):
    top = terms[0]
    for t in terms[1:]:
        top = jnp.maximum(top, t)
    sums = None
    for t in terms:
        term = t * pltpu.roll(jnp.exp(t - top), 4, axis=0)
        sums = term if sums is None else sums + term
    return jnp.where(lax.broadcasted_iota(jnp.int32, top.shape, 0) < 4, top, sums)


def kernel(
    lat, gr, cb, hc, olat, ocb,
    LAT, GR, HC, HCL, CB, CBT, E, PU, D, H, ST, SC, SCR, SY, SZ, FIN,
    GCT, GCR, GYK, GYT, GYR, GZT, GZR, GA, GXT, GXR, OC,
    ss, rs, ls,
):
    T, W = lat.shape
    K = cb.shape[0]
    half = T // 2
    part = T // 16
    dp = lax.axis_index("dp")
    code = lax.axis_index("code")
    c = dp % NC
    z = dp // NC % NZ
    yl = dp // (NC * NZ)
    x = code // 2
    yh = code % 2
    y = yh * 2 + yl
    zb = z // 4
    zt = xor4(z % 4, x)

    def at(dx=0, dy=0, dz=0, dc=0):
        return device((x + dx) % NX, (y + dy) % NY, (z + dz) % NZ, (c + dc) % NC)

    def diag(dz):
        z_ = (z + dz) % NZ
        return device(xor4(x, xor4(z % 4, z_ % 4)), y, z_, c)

    def copy(src, dst, dev, i, j=None):
        return pltpu.make_async_remote_copy(
            src_ref=src, dst_ref=dst, send_sem=ss.at[i], recv_sem=rs.at[i if j is None else j],
            device_id=dev, device_id_type=MESH,
        )

    def send(src, dst, dev, i, j=None):
        copy(src, dst, dev, i, j).start()

    def recv(dst, i):
        copy(dst, dst, at(dc=1), i).wait_recv()

    def sent(src, i):
        copy(src, src, at(dc=1), i).wait_send()

    def codes(j, first=0, count=K):
        return pl.ds(pl.multiple_of(j * K + first, count), count)

    xh = [(dx, dh) for dx in range(NX) for dh in range(2)]

    def across(dx, dh):
        return device((x + dx) % NX, (yh + dh) % 2 * 2 + yl, z, c)

    barrier = pltpu.get_barrier_semaphore()

    def greet(dev):
        pl.semaphore_signal(barrier, inc=1, device_id=dev, device_id_type=MESH)

    away = [jnp.logical_not((x == 0) & (zb == b)) for b in range(2)]
    home = (x == 0) & (zb == yh)
    for d in range(1, NX):
        greet(at(dx=d))
    greet(at(dc=1))
    for d in range(1, NY):
        greet(at(dy=d))
    for d in range(1, NZ):
        greet(diag(d))
    for dx, dh in xh[1:]:
        greet(across(dx, dh))
    for b in range(2):
        @pl.when(away[b])
        def _(b=b):
            greet(device(x, y, zt + 4 * b, c))
    for zs in range(NZ):
        @pl.when(jnp.logical_not(home & (z == zs)))
        def _(zs=zs):
            greet(device(xor4(zs % 4, z % 4), zb * 2 + yl, zs, c))

    peers = NX - 1 + 1 + NY - 1 + NZ - 1 + 7 + 2 + 8
    peers = peers - jnp.where(x == 0, 1, 0) - jnp.where(home, 1, 0)
    pl.semaphore_wait(barrier, peers)

    def tile(h_, c_, yl_):
        return (h_ * 2 + c_) * 2 + yl_

    def tokens(q):
        return pl.ds(pl.multiple_of(q * T, T), T)

    def half_rows(h_, c_, yl_, b_):
        return pl.ds(pl.multiple_of(tile(h_, c_, yl_) * T + b_ * half, half), half)

    def pieces(c_, yl_, b_):
        for h_ in range(2):
            rows = half_rows(h_, c_, yl_, b_)
            yield LAT.at[rows]
            yield GR.at[rows]
        yield HC.at[(c_ * 2 + yl_) * 2 + b_]

    first_half, second_half = pl.ds(0, K // 2), pl.ds(K // 2, K // 2)
    send(cb.at[first_half], CB.at[codes(x, 0, K // 2)], at(dx=1), S_X)
    send(cb.at[second_half], CB.at[codes(x, K // 2, K // 2)], at(dx=NX - 1), S_X + 2)

    HCL[...] = jnp.broadcast_to(hc[...].reshape(1, T), (8, T))
    own = [arr.at[pl.ds(h * half, half)] for h in range(2) for arr in (lat, gr)] + [HCL]
    dst = list(pieces(c, yl, zb))
    for p in range(5):
        for b in range(2):
            @pl.when(away[b])
            def _(p=p, b=b):
                send(own[p], dst[p], device(x, y, zt + 4 * b, c), S_Z + b * 5 + p, S_Z + zb * 5 + p)
        if p == 1:
            send(cb.at[second_half], CB.at[codes(x, K // 2, K // 2)], at(dx=1), S_X + 1)
            send(cb.at[first_half], CB.at[codes(x, 0, K // 2)], at(dx=NX - 1), S_X + 3)

    def local(src, dst, i):
        return pltpu.make_async_copy(src, dst, ls.at[i])

    keep = [local(own[p], dst[p], p) for p in range(4)]
    keep_codes = local(cb, CB.at[codes(x)], 4)
    keep_codes.start()

    @pl.when(x == 0)
    def _():
        for one in keep:
            one.start()
        HC[(c * 2 + yl) * 2 + zb] = HCL[...]

    groups = [(c_, yl_) for c_ in (c, 1 - c) for yl_ in (yl, 1 - yl)]
    refs = [list(pieces(c_, yl_, b)) for c_, yl_ in groups for b in range(2)]
    left = (x + NX - 1) % NX
    right = (x + 1) % NX
    far = (x + 2) % NX
    far_refs = [CB.at[codes(left, 0, K // 2)], CB.at[codes(right, K // 2, K // 2)]]

    def from_z(p):
        for b in range(2):
            ref = refs[b][p]

            @pl.when(away[b])
            def _(ref=ref, i=S_Z + b * 5 + p):
                recv(ref, i)

            if p < 4:
                @pl.when(jnp.logical_not(away[b]))
                def _():
                    keep[p].wait()

            send(ref, ref, at(dy=NY - 1 if b else 1), (S_YB if b else S_YA) + p)
            send(ref, ref, at(dc=1), S_C + 5 * b + p)

    def from_y(p):
        for b in range(2):
            ref = refs[2 + b][p]
            recv(ref, (S_YB if b else S_YA) + p)
            send(ref, ref, at(dc=1), S_C + 10 + 5 * b + p)

    def from_core(p):
        for k in range(4):
            recv(refs[4 + k][p], S_C + 5 * k + p)

    from_z(0)
    recv(far_refs[0], S_X)
    send(far_refs[0], far_refs[0], at(dx=1), S_X + 4)
    recv(far_refs[1], S_X + 2)
    send(far_refs[1], far_refs[1], at(dx=NX - 1), S_X + 5)
    from_z(1)
    from_y(0)
    from_z(2)
    from_y(1)
    recv(CB.at[codes(left, K // 2, K // 2)], S_X + 1)
    recv(CB.at[codes(right, 0, K // 2)], S_X + 3)
    recv(CB.at[codes(far, 0, K // 2)], S_X + 4)
    recv(CB.at[codes(far, K // 2, K // 2)], S_X + 5)
    keep_codes.wait()

    def first(n):
        q = order[n]
        logit = nt_dot(CB[...], LAT[tokens(q), :])
        E[n] = logit
        PU[n] = nt_dot(CB[...], GR[tokens(q), :])
        top = jnp.max(logit, axis=0, keepdims=True)

        def rows(i, sums):
            at_ = pl.ds(pl.multiple_of(i * STEP, STEP), STEP)
            expo = jnp.exp(E[n, at_, :] - top)
            E[n, at_, :] = expo
            weighted = expo * PU[n, at_, :]
            return (
                sums[0] + jnp.sum(expo.reshape(STEP // 8, 8, T), axis=0),
                sums[1] + jnp.sum(weighted.reshape(STEP // 8, 8, T), axis=0),
            )

        zero = jnp.zeros((8, T), F32)
        total, weighted = lax.fori_loop(0, NX * K // STEP, rows, (zero, zero))
        total = jnp.sum(total, axis=0, keepdims=True)
        weighted = jnp.sum(weighted, axis=0, keepdims=True)
        ST[q] = jnp.concatenate([top, total, weighted, jnp.zeros((5, T), F32)], axis=0)

    order = [tile(h, c_, yl_) for h in range(2) for c_, yl_ in groups]

    def both(h, c_):
        one, two = ST[tile(h, c_, 0)], ST[tile(h, c_, 1)]
        tops = [one[0:1], two[0:1]]
        return jnp.concatenate([*tops, *tops, one[1:2], two[1:2], one[2:3], two[2:3]], axis=0)

    def stats_core(h):
        SC[h] = both(h, 1 - c)
        send(SC.at[h], SCR.at[h], at(dc=1), S_SC + h)

    def stats_y(h):
        mine = both(h, c)
        recv(SCR.at[h], S_SC + h)
        SY[h, 0] = merge([mine, SCR[h]])
        for d in range(1, NY):
            send(SY.at[h, 0], SY.at[h, d], at(dy=d), S_SY + 4 * h + d)

    def stats_z(h):
        for d in range(1, NY):
            recv(SY.at[h, d], S_SY + 4 * h + d)
        SZ[h, 0] = merge([SY[h, d] for d in range(NY)])
        for d in range(1, NZ):
            send(SZ.at[h, 0], SZ.at[h, d], diag(d), S_SZ + 8 * h + d)

    def stats_last(h):
        for d in range(1, NZ):
            recv(SZ.at[h, d], S_SZ + 8 * h + d)
        FIN[h, c] = merge([SZ[h, d] for d in range(NZ)])
        send(FIN.at[h, c], FIN.at[h, c], at(dc=1), S_SF + h)

    def stats_end(h):
        recv(FIN.at[h, 1 - c], S_SF + h)

    base = ((yl * NZ + z) * NC + c) * 8 + yh

    def hard_rows(d):
        first_code = (base + (x + d) % NX * 2) * K
        ids = first_code + lax.broadcasted_iota(jnp.int32, (K, 8 * T), 0)
        row = jnp.concatenate(
            [HC[g * 2 + b][0:1, h * half:(h + 1) * half] for h in range(2) for g in range(4) for b in range(2)],
            axis=1,
        )
        hit = jnp.where(row == ids, 1.0, 0.0).astype(BF16)
        H[d] = jnp.dot(hit, GR[...], preferred_element_type=F32)

    def latent_grad(n):
        q = order[n]
        pair = FIN[n // 4, q // 2 % 2]
        fin = jnp.where(q % 2 == 0, pair, pltpu.roll(pair, 7, axis=0))
        inverse = 1.0 / fin[4:5]
        factor = jnp.exp(ST[q][0:1] - fin[0:1]) * inverse
        dlog = ((E[n] * factor) * (PU[n] - fin[6:7] * inverse)).astype(BF16)
        D[:, tokens(q)] = dlog
        return jnp.dot(CBT[...], dlog, preferred_element_type=F32).T

    def latent_other(h):
        for k in range(2):
            GCT[h, k] = latent_grad(4 * h + 2 + k)
            send(GCT.at[h, k], GCR.at[h, k], at(dc=1), S_GC + 2 * h + k)

    def latent_own(h):
        for k in (1, 0):
            total = latent_grad(4 * h + k)
            recv(GCR.at[h, k], S_GC + 2 * h + k)
            GYK[h, k] = total + GCR[h, k]
            GYT[h, k] = GYK[h, k].astype(BF16)

            def part_of(b):
                return GYT.at[h, k, pl.ds(pl.multiple_of(b * half, half), half)]

            if k:
                for b in range(2):
                    dev = device(x, b * 2 + 1 - yl, z, c)
                    send(part_of(b), GYR.at[h, y], dev, S_GY + 4 * h + b, S_GY + 4 * h + y)
            else:
                send(part_of(1 - yh), GYR.at[h, y], at(dy=2), S_GY + 4 * h + 2, S_GY + 4 * h + y)

    def rows_of(x_, yh_, first=0):
        return pl.ds(pl.multiple_of(first + (x_ * 2 + yh_) * part, part), part)

    def latent_home(h):
        total = GYK[h, 0, pl.ds(pl.multiple_of(yh * half, half), half), :]
        for d in range(1, NY):
            y_ = (y + d) % NY
            recv(GYR.at[h, y_], S_GY + 4 * h + y_)
            total = total + GYR[h, y_].astype(F32)
        GZT[h] = total.astype(BF16)
        for dx, dh in xh:
            x_ = (x + dx) % NX
            yh_ = (yh + dh) % 2
            src = GZT.at[h, rows_of(x_, yh_)]
            dev = device(x_, yh_ * 2 + yl, zt + 4 * yh, c)
            if dx or dh:
                send(src, GZR.at[h, z], dev, S_GZ + 8 * h + dx * 2 + dh, S_GZ + 8 * h + z)
            else:
                @pl.when(jnp.logical_not(home))
                def _(src=src, dev=dev):
                    send(src, GZR.at[h, z], dev, S_GZ + 8 * h, S_GZ + 8 * h + z)

                @pl.when(home)
                def _():
                    GZR[h, z] = GZT[h, rows_of(x, yh), :]

    def latent_spread(h):
        for zs in range(NZ):
            @pl.when(jnp.logical_not(home & (z == zs)))
            def _(zs=zs):
                recv(GZR.at[h, zs], S_GZ + 8 * h + zs)
        total = GZR[h, 0].astype(F32)
        for zs in range(1, NZ):
            total = total + GZR[h, zs].astype(F32)
        rows = rows_of(x, yh, h * half)
        GA[h] = total
        for dx, dh in xh[1:]:
            send(GA.at[h], olat.at[rows], across(dx, dh), S_AG + 8 * h + dx * 2 + dh)
        local(GA.at[h], olat.at[rows], 5 + h).start()

    def codebook_grad(d):
        return H[d] + jnp.dot(D[codes((x + d) % NX), :], LAT[...], preferred_element_type=F32)

    def codebook_send(d):
        GXT[d] = codebook_grad(d).astype(BF16)
        send(GXT.at[d], GXR.at[d], at(dx=d), S_GX + d)

    first(0)
    from_z(3)
    from_core(0)
    from_core(1)
    first(1)
    from_y(2)
    from_z(4)
    first(2)
    first(3)
    stats_core(0)
    from_y(3)
    from_y(4)
    first(4)
    stats_y(0)
    first(5)
    for p in range(2, 5):
        from_core(p)
    first(6)
    stats_z(0)
    first(7)
    stats_core(1)
    hard_rows(2)
    stats_y(1)
    hard_rows(1)
    hard_rows(3)
    CBT[...] = CB[...].T
    stats_last(0)
    stats_z(1)
    stats_end(0)
    latent_other(0)
    latent_own(0)
    hard_rows(0)
    stats_last(1)
    stats_end(1)
    latent_other(1)
    latent_home(0)
    latent_own(1)
    codebook_send(2)
    latent_home(1)
    latent_spread(0)
    codebook_send(1)
    codebook_send(3)
    latent_spread(1)
    total = codebook_grad(0)
    for d in range(1, NX):
        recv(GXR.at[d], S_GX + d)
        total = total + GXR[d].astype(F32)
    OC[...] = total
    out = local(OC, ocb, 7)
    out.start()

    for h in range(2):
        for dx, dh in xh[1:]:
            rows = rows_of((x + NX - dx) % NX, (yh + dh) % 2, h * half)
            recv(olat.at[rows], S_AG + 8 * h + dx * 2 + dh)
        local(GA.at[h], olat.at[rows_of(x, yh, h * half)], 5 + h).wait()
    out.wait()

    for n in range(4):
        sent(cb.at[first_half], S_X + n)
    sent(far_refs[0], S_X + 4)
    sent(far_refs[1], S_X + 5)
    for p in range(5):
        for b in range(2):
            @pl.when(away[b])
            def _(p=p, b=b):
                sent(own[p], S_Z + b * 5 + p)

        sent(refs[0][p], S_YA + p)
        sent(refs[1][p], S_YB + p)
        for k in range(4):
            sent(refs[k][p], S_C + 5 * k + p)
    for h in range(2):
        sent(SC.at[h], S_SC + h)
        sent(SC.at[h], S_SF + h)
        for d in range(1, NY):
            sent(SC.at[h], S_SY + 4 * h + d)
        for d in range(1, NZ):
            sent(SC.at[h], S_SZ + 8 * h + d)
        for k in range(2):
            sent(GCT.at[h, k], S_GC + 2 * h + k)
        for n in range(3):
            sent(GYR.at[0, 0], S_GY + 4 * h + n)
        for n in range(1, 8):
            sent(GZR.at[0, 0], S_GZ + 8 * h + n)
            sent(GA.at[h], S_AG + 8 * h + n)

        @pl.when(jnp.logical_not(home))
        def _(h=h):
            sent(GZR.at[0, 0], S_GZ + 8 * h)
    for d in range(1, NX):
        sent(GXT.at[d], S_GX + d)


def per_device(latents, grads, codebook, hard_code):
    T, W = latents.shape
    K = codebook.shape[0]
    part = T // 16
    half = T // 2
    vmem = pl.BlockSpec(memory_space=pltpu.VMEM)
    hbm = pl.BlockSpec(memory_space=pl.ANY)
    scratch = [
        ((8 * T, W), BF16),
        ((8 * T, W), BF16),
        ((8, 8, T), jnp.int32),
        ((8, T), jnp.int32),
        ((NX * K, W), BF16),
        ((W, NX * K), BF16),
        ((8, NX * K, T), F32),
        ((8, NX * K, T), F32),
        ((NX * K, 8 * T), BF16),
        ((NX, K, W), F32),
        ((8, 8, T), F32),
        ((2, 8, T), F32),
        ((2, 8, T), F32),
        ((2, NY, 8, T), F32),
        ((2, NZ, 8, T), F32),
        ((2, 2, 8, T), F32),
        ((2, 2, T, W), F32),
        ((2, 2, T, W), F32),
        ((2, 2, T, W), F32),
        ((2, 2, T, W), BF16),
        ((2, 4, half, W), BF16),
        ((2, half, W), BF16),
        ((2, NZ, part, W), BF16),
        ((2, part, W), F32),
        ((NX, K, W), BF16),
        ((NX, K, W), BF16),
        ((K, W), F32),
    ]
    return pl.pallas_call(
        kernel,
        out_shape=(jax.ShapeDtypeStruct((T, W), F32), jax.ShapeDtypeStruct((K, W), F32)),
        in_specs=[hbm, hbm, hbm, vmem],
        out_specs=(hbm, hbm),
        scratch_shapes=[pltpu.VMEM(s, t) for s, t in scratch]
        + [pltpu.SemaphoreType.DMA((n,)) for n in (S_ALL, S_ALL, 8)],
        compiler_params=pltpu.CompilerParams(
            collective_id=0, has_side_effects=True, vmem_limit_bytes=62 * 2**20
        ),
    )(latents, grads, codebook, hard_code)


def solution(mesh):
    return jax.shard_map(
        per_device,
        mesh=mesh,
        in_specs=(P("dp", None), P("dp", None), P(("dp", "code"), None), P("dp")),
        out_specs=(P("dp", None), P(("dp", "code"), None)),
        check_vma=False,
    )
```

time: 90.5 us -> 82.9 us (0.916)
  the two profiles are of different devices: /device:TPU:32 before, /device:TPU:1 now
where the time goes in v3:
time: 82.9 us; the launch traced here: 82.7 us
  Pallas kernels  79.6 us (96%)
  local copies, waits for them, and re-layouts  2.52 us (3%)
    pallas_call x1, Pallas kernels, per_device(): pl.pallas_call(kernel, out_shape=(jax.ShapeDtypeStruct((T, W), F32), jax....  79.6 us
    unnamed x4, local copies, waits for them, and re-layouts  2.52 us

profile of v3, /device:TPU:1, one launch (start us, length us, event | category | flops | bytes accessed | tf_op | source)
XLA Modules:
  0.0 82.7 jit_solution(11669656827251757611)
XLA Ops:
  0.6 79.6 %shard_map.59 = (f32[256,256]{1,0:T(8,128)}, f32[512,256]{1,0:T(8,128)}) custom-call(bf16[256,256]{1,0:T(8,128)(2,1)} %lat.1, bf16[256,256]{1,0:T(8,128)(2,1)} %gr.1, bf16[512,256]{1,0:T(8,128)(2,1)} %cb.1, s32[256]{0:T(256)} %hc.1), custom_call_target="tpu_custom_call" | custom-call | tf_op jit(solution)/shard_map/pallas_call | solution.py:508
  80.2 0.0 copy-start
  80.2 1.7 %copy.8 = f32[256,256]{1,0:T(8,128)} copy(f32[256,256]{1,0:T(8,128)} %get-tuple-element.4) | data formatting | bytes 524288
  81.9 0.0 copy-done
  81.9 0.8 copy.9
Async XLA Ops:
  80.2 1.7 %copy-start = (f32[512,256]{1,0:T(8,128)S(1)}, f32[512,256]{1,0:T(8,128)}, u32[]{:S(2)}) copy-start(f32[512,256]{1,0:T(8,128)} %get-tuple-element.5) | copy-start | bytes 1572868

commit v4 on v3

--- a/solution.py
+++ b/solution.py
@@ -371,8 +371,17 @@
     def codebook_grad(d):
         return H[d] + jnp.dot(D[codes((x + d) % NX), :], LAT[...], preferred_element_type=F32)
 
+    def codebook_far():
+        GXT[2] = codebook_grad(2).astype(BF16)
+        send(GXT.at[2, first_half], GXR.at[2, first_half], at(dx=1), S_GX)
+        send(GXT.at[2, second_half], GXR.at[2, second_half], at(dx=3), S_GX + 2)
+
     def codebook_send(d):
-        GXT[d] = codebook_grad(d).astype(BF16)
+        rows = first_half if d == 1 else second_half
+        OC[...] = codebook_grad(d)
+        recv(GXR.at[2, rows], S_GX + d - 1)
+        OC[rows, :] = OC[rows, :] + GXR[2, rows, :].astype(F32)
+        GXT[d] = OC[...].astype(BF16)
         send(GXT.at[d], GXR.at[d], at(dx=d), S_GX + d)
 
     first(0)
@@ -412,14 +421,14 @@
     latent_other(1)
     latent_home(0)
     latent_own(1)
-    codebook_send(2)
+    codebook_far()
     latent_home(1)
     latent_spread(0)
     codebook_send(1)
     codebook_send(3)
     latent_spread(1)
     total = codebook_grad(0)
-    for d in range(1, NX):
+    for d in (1, 3):
         recv(GXR.at[d], S_GX + d)
         total = total + GXR[d].astype(F32)
     OC[...] = total
@@ -465,7 +474,8 @@
         @pl.when(jnp.logical_not(home))
         def _(h=h):
             sent(GZR.at[0, 0], S_GZ + 8 * h)
-    for d in range(1, NX):
+    for d in (1, 3):
+        sent(GXT.at[2, first_half], S_GX + d - 1)
         sent(GXT.at[d], S_GX + d)
 
 

time: 82.9 us -> 81.1 us (0.978)
  the two profiles are of different devices: /device:TPU:1 before, /device:TPU:32 now
where the time goes in v4:
time: 81.1 us; the launch traced here: 80.9 us
  Pallas kernels  77.8 us (96%)
  local copies, waits for them, and re-layouts  2.52 us (3%)
    pallas_call x1, Pallas kernels, per_device(): pl.pallas_call(kernel, out_shape=(jax.ShapeDtypeStruct((T, W), F32), jax....  77.8 us
    unnamed x4, local copies, waits for them, and re-layouts  2.52 us

profile of v4, /device:TPU:32, one launch (start us, length us, event | category | flops | bytes accessed | tf_op | source)
XLA Modules:
  0.0 80.9 jit_solution(3314313328632944490)
XLA Ops:
  0.6 77.8 %shard_map.59 = (f32[256,256]{1,0:T(8,128)}, f32[512,256]{1,0:T(8,128)}) custom-call(bf16[256,256]{1,0:T(8,128)(2,1)} %lat.1, bf16[256,256]{1,0:T(8,128)(2,1)} %gr.1, bf16[512,256]{1,0:T(8,128)(2,1)} %cb.1, s32[256]{0:T(256)} %hc.1), custom_call_target="tpu_custom_call" | custom-call | tf_op jit(solution)/shard_map/pallas_call | solution.py:518
  78.4 0.0 copy-start
  78.4 1.7 %copy.8 = f32[256,256]{1,0:T(8,128)} copy(f32[256,256]{1,0:T(8,128)} %get-tuple-element.4) | data formatting | bytes 524288
  80.1 0.0 copy-done
  80.1 0.8 copy.9
Async XLA Ops:
  78.4 1.7 %copy-start = (f32[512,256]{1,0:T(8,128)S(1)}, f32[512,256]{1,0:T(8,128)}, u32[]{:S(2)}) copy-start(f32[512,256]{1,0:T(8,128)} %get-tuple-element.5) | copy-start | bytes 1572868

commit v5 on v4

--- a/solution.py
+++ b/solution.py
@@ -479,6 +479,18 @@
         sent(GXT.at[d], S_GX + d)
 
 
+def place(one, two, out_one, out_two, sems):
+    copies = []
+    for src, dst in ((one, out_one), (two, out_two)):
+        for first in range(0, src.shape[0], 128):
+            rows = pl.ds(first, 128)
+            copies.append(pltpu.make_async_copy(src.at[rows], dst.at[rows], sems.at[len(copies)]))
+    for one_copy in copies:
+        one_copy.start()
+    for one_copy in copies:
+        one_copy.wait()
+
+
 def per_device(latents, grads, codebook, hard_code):
     T, W = latents.shape
     K = codebook.shape[0]
@@ -515,7 +527,7 @@
         ((NX, K, W), BF16),
         ((K, W), F32),
     ]
-    return pl.pallas_call(
+    results = pl.pallas_call(
         kernel,
         out_shape=(jax.ShapeDtypeStruct((T, W), F32), jax.ShapeDtypeStruct((K, W), F32)),
         in_specs=[hbm, hbm, hbm, vmem],
@@ -526,6 +538,13 @@
             collective_id=0, has_side_effects=True, vmem_limit_bytes=62 * 2**20
         ),
     )(latents, grads, codebook, hard_code)
+    return pl.pallas_call(
+        place,
+        out_shape=(jax.ShapeDtypeStruct((T, W), F32), jax.ShapeDtypeStruct((K, W), F32)),
+        in_specs=[hbm, hbm],
+        out_specs=(hbm, hbm),
+        scratch_shapes=[pltpu.SemaphoreType.DMA((6,))],
+    )(*results)
 
 
 def solution(mesh):

time: 81.1 us -> 104 us (1.28)
  Pallas kernels: 77.8 us -> 103 us
  local copies, waits for them, and re-layouts: 2.52 us -> 0 us
    pallas_call x0 -> x1, Pallas kernels: none -> 25 us  [per_device(): pl.pallas_call(place, out_shape=(jax.ShapeDtypeStruct((T, W), F32), jax.S...]
    unnamed x4 -> x0, local copies, waits for them, and re-layouts: 2.52 us -> none
where the time goes in v5:
time: 104 us
  Pallas kernels  103 us (99%)
    pallas_call x1, Pallas kernels, per_device(): pl.pallas_call(kernel, out_shape=(jax.ShapeDtypeStruct((T, W), F32), jax....  77.8 us
    pallas_call x1, Pallas kernels, per_device(): pl.pallas_call(place, out_shape=(jax.ShapeDtypeStruct((T, W), F32), jax.S...  25 us

profile of v5, /device:TPU:32, one launch (start us, length us, event | category | flops | bytes accessed | tf_op | source)
XLA Modules:
  0.0 103.5 jit_solution(7142401401583867021)
XLA Ops:
  0.6 77.8 %shard_map.59 = (f32[256,256]{1,0:T(8,128)}, f32[512,256]{1,0:T(8,128)}) custom-call(bf16[256,256]{1,0:T(8,128)(2,1)} %lat.1, bf16[256,256]{1,0:T(8,128)(2,1)} %gr.1, bf16[512,256]{1,0:T(8,128)(2,1)} %cb.1, s32[256]{0:T(256)} %hc.1), custom_call_target="tpu_custom_call" | custom-call | tf_op jit(solution)/shard_map/pallas_call | solution.py:530
  78.4 25.0 %shard_map.60 = (f32[256,256]{1,0:T(8,128)}, f32[512,256]{1,0:T(8,128)}) custom-call(f32[256,256]{1,0:T(8,128)} %get-tuple-element.4.one, f32[512,256]{1,0:T(8,128)} %get-tuple-element.5.two), custom_call_target="tpu_custom_call" | custom-call | tf_op jit(solution)/shard_map/pallas_call | solution.py:541
